TPU v7x, 32 devices: a whole 2x2x4 slice. The times are simulated.
32 devices in a mesh: rows: 8 (over z, y), serve: 4 (over x, core).
Axes of the slice: x: 2, y: 2, z: 4, core: 2. Of those that a mesh axis runs over, the one named last changes fastest.
Arguments:
- rows_small: float32 [32768, 32], P(('rows', 'serve')), may hold values from -6 to 6
- rows_mid: float32 [32768, 64], P(('rows', 'serve')), may hold values from -6 to 6
- rows_wide: float32 [32768, 128], P(('rows', 'serve')), may hold values from -6 to 6
- row_grads: float32 [3, 32768, 256], P(None, ('rows', 'serve'))
- proj_small: float32 [32, 256], replicated, may hold values from -1 to 1
- proj_mid: float32 [64, 256], replicated, may hold values from -0.75 to 0.75
- proj_wide: float32 [128, 256], replicated, may hold values from -0.5 to 0.5
- counts: int32 [3, 32], P(None, ('rows', 'serve')), may hold values from 512 to 1024, as said below
- owners: int32 [3, 32768, 1], P(None, ('rows', 'serve')), may hold values from 0 to 31; in each aligned block of 1024 rows (0 to 1023, 1024 to 2047, ..., all dimensions but the last counted through in order) at most 48 rows name the same one
Outputs:
- served: bfloat16 [49152, 768], P(('rows', 'serve'))
Inputs may be any that keep to these rules, and one draw needn't show every extreme that they name: `counts`: one device of each tier has all 1024 slots live. `owners`: among the 1024 slots of one device and tier at most 48 name one owner, and exactly 48 do for some owner.
All inputs are finite; a program needn't handle non-finite values.
Results may differ from a plain program's by a relative error of at most 0.001.
Values may be sent and summed in bfloat16 or wider, within the bound.
No kernel may reach another device: no remote copies, remote signals or barrier semaphores. Data moves between devices by JAX's collectives and lax.ppermute only.
A program may use at most 64 MiB of HBM per device.

v0:
```python
import jax
import jax.numpy as jnp
from jax import lax
from jax.sharding import PartitionSpec as P

STEP_NORM = 16.0
ROW_RATE = 0.1


def refresh_factor(total):
    return STEP_NORM / jnp.sqrt(jnp.sum(total * total) + 1e-06)


def highest_dot(left, right):
    return jnp.dot(left, right, precision=lax.Precision.HIGHEST, preferred_element_type=jnp.float32)


def owner_slots(owner, valid, device_count, capacity):
    columns = jnp.arange(device_count, dtype=jnp.int32)
    matched = (owner[:, None] == columns[None, :]) & valid[:, None]
    hit_counts = matched.astype(jnp.int32)
    before = jnp.cumsum(hit_counts, axis=0) - hit_counts
    slot_index = jnp.sum(jnp.where(matched, before, 0), axis=1)
    return jnp.where(valid, owner * capacity + slot_index, device_count * capacity)


def place_rows(values, target, device_count, capacity):
    empty = jnp.zeros((device_count * capacity, values.shape[1]), values.dtype)
    return empty.at[target].set(values, mode="drop")


def sum_gradients(totals):
    return lax.psum((totals[0], totals[1], totals[2]), ("rows", "serve"))


def route_projected(buffer):
    return lax.all_to_all(buffer, ("rows", "serve"), split_axis=0, concat_axis=0, tiled=True)


def local(
    rows_small, rows_mid, rows_wide, row_grads, proj_small, proj_mid, proj_wide, counts, owners
):
    device_count = lax.axis_size("rows") * lax.axis_size("serve")
    slots_here = rows_small.shape[0]
    capacity = max(2, slots_here // device_count + slots_here // (2 * device_count))
    out_width = row_grads.shape[2]
    tables = (rows_small, rows_mid, rows_wide)
    projections = (proj_small, proj_mid, proj_wide)
    positions = jnp.arange(slots_here, dtype=jnp.int32)
    new_rows = []
    targets = []
    totals = []
    for tier_index in range(3):
        valid = positions < counts[tier_index, 0]
        gradients = jnp.where(valid[:, None], row_grads[tier_index], 0.0)
        totals.append(highest_dot(tables[tier_index].T, gradients))
        row_step = highest_dot(gradients, projections[tier_index].T)
        new_rows.append(tables[tier_index] - ROW_RATE * row_step)
        targets.append(owner_slots(owners[tier_index, :, 0], valid, device_count, capacity))
    summed = sum_gradients(totals)
    projected = []
    for tier_index in range(3):
        new_proj = projections[tier_index] - refresh_factor(summed[tier_index]) * summed[tier_index]
        projected.append(highest_dot(new_rows[tier_index], new_proj).astype(jnp.bfloat16))
    blocks = [
        place_rows(projected[tier_index], targets[tier_index], device_count, capacity)
        for tier_index in range(3)
    ]
    outgoing = jnp.concatenate(blocks, axis=1).reshape(device_count, capacity * 3 * out_width)
    moved = route_projected(outgoing)
    return moved.reshape(device_count * capacity, 3 * out_width)


def solution(mesh):
    return jax.shard_map(
        local,
        mesh=mesh,
        in_specs=(
            P(("rows", "serve"), None),
            P(("rows", "serve"), None),
            P(("rows", "serve"), None),
            P(None, ("rows", "serve"), None),
            P(),
            P(),
            P(),
            P(None, ("rows", "serve")),
            P(None, ("rows", "serve"), None),
        ),
        out_specs=P(("rows", "serve"), None),
        check_vma=False,
    )
```

profile of v0, /device:TPU:0, one launch (start us, length us, event | category | flops | bytes accessed | tf_op | source)
XLA Modules:
  0.0 282.1 jit_solution(17468594121481000078)
XLA Ops:
  6.5 1.5 fusion.58
  9.9 2.7 convolution_bitcast_fusion.1
  12.6 4.0 %convolution_bitcast_fusion = f32[128,256]{0,1:T(8,128)} fusion(f32[1024,128]{1,0:T(8,128)} %param.11, f32[3,1024,256]{2,1,0:T(8,128)} %param.12, pred[1024]{0:T(1024)(128)(4,1)S(1)} %iota_compare_fusion.6), kind=kOutput, calls=%fused_computation.13 | convolution fusion | flops 402915328 | bytes 1704960 | tf_op jit(solution)/shard_map/dot_general | solution.py:15
  20.2 42.1 %psum.21 = f32[32,256]{1,0:T(8,128)S(1)} all-reduce(f32[32,256]{1,0:T(8,128)S(1)} %convolution_bitcast_fusion.2), channel_id=1, replica_groups=mesh['rows'=8,'serve'=4] {'rows','serve'}, use_global_device_ids=true, to_apply=%region_3.4 | all-reduce | flops 8192 | bytes 65536 | tf_op jit(solution)/shard_map/psum | solution.py:33
  63.7 9.0 %reduce-window.24 = s32[32,8,128]{2,1,0:T(8,128)S(1)} reduce-window(s32[32,8,128]{2,1,0:T(8,128)S(1)} %fusion.37, s32[]{:T(128)} %constant.12.clone.1), window={size=1x1x128 pad=0_0x0_0x127_0}, to_apply=%region_6.7 | reduce-window | flops 4161536 | bytes 262148 | tf_op jit(solution)/shard_map/reduce-window.2
  72.7 9.0 %reduce-window.26 = s32[32,8,128]{2,1,0:T(8,128)S(1)} reduce-window(s32[32,8,128]{2,1,0:T(8,128)S(1)} %fusion.40, s32[]{:T(128)} %constant.12.clone.1), window={size=1x1x128 pad=0_0x0_0x127_0}, to_apply=%region_12.13 | reduce-window | flops 4161536 | bytes 262148 | tf_op jit(solution)/shard_map/reduce-window.4
  82.4 15.7 %reduce-window.20 = s32[32,8,128]{2,1,0:T(8,128)S(1)} reduce-window(s32[32,8,128]{2,1,0:T(8,128)} %fusion.34, s32[]{:T(128)} %constant.12.clone.1), window={size=1x1x128 pad=0_0x0_0x127_0}, to_apply=%region_0.1 | reduce-window | flops 4161536 | bytes 262148 | tf_op jit(solution)/shard_map/reduce-window
  98.8 1.6 copy.25
  103.3 2.1 fusion.2
  106.2 1.0 copy.29
  111.7 2.2 fusion.1
  114.0 3.0 %fusion = f32[1024,128]{1,0:T(8,128)} fusion(f32[1024,128]{1,0:T(8,128)} %param.11, f32[128,256]{1,0:T(8,128)} %param.15, f32[3,1024,256]{2,1,0:T(8,128)S(1)} %copy-done, pred[1024]{0:T(1024)(128)(4,1)} %copy-done.10), kind=kOutput, calls=%fused_computation.8 | convolution fusion | flops 403177472 | bytes 2229248 | tf_op jit(solution)/shard_map/dot_general | solution.py:15
  116.9 1.0 fusion.29
  119.9 1.8 convolution_convert_fusion.2
  121.7 2.0 compare_select_fusion.2
  123.6 1.0 copy.31
  124.6 5.4 %scatter_custom_fusion = bf16[1536,256]{1,0:T(8,128)(2,1)S(1)} fusion(s32[1024]{0:T(1024)S(1)} %bitcast.128, bf16[1024,256]{1,0:T(8,128)(2,1)S(1)} %convolution_convert_fusion.2, bf16[]{:T(256)} %constant.9.clone.1), kind=kCustom, calls=%fused_computation.35 | custom fusion | bytes 786434 | tf_op jit(solution)/shard_map/scatter | solution.py:29
  130.0 13.2 %all-reduce.3.cloned.1.call-done = (f32[128,256]{0,1:T(8,128)}, f32[64,256]{1,0:T(8,128)}) async-done(((f32[128,256]{0,1:T(8,128)}, f32[64,256]{1,0:T(8,128)}), (f32[128,256]{0,1:T(8,128)}, f32[64,256]{1,0:T(8,128)})) %all-reduce.3.cloned.1.call-update) | async-done | bytes 196624 | tf_op jit(solution)/shard_map/psum | solution.py:33
  143.2 1.5 multiply_reduce_fusion.1
  145.3 1.5 multiply_reduce_fusion
  147.4 1.9 convolution_convert_fusion.1
  149.3 5.9 %scatter_custom_fusion.1 = bf16[1536,256]{1,0:T(8,128)(2,1)} fusion(s32[1024]{0:T(1024)S(1)} %bitcast.127, bf16[1024,256]{1,0:T(8,128)(2,1)S(1)} %convolution_convert_fusion.1, bf16[]{:T(256)} %constant.9.clone.1), kind=kCustom, calls=%fused_computation.33 | custom fusion | bytes 786434 | tf_op jit(solution)/shard_map/scatter | solution.py:29
  155.2 1.9 convolution_convert_fusion
  157.1 5.9 %scatter_custom_fusion.2 = bf16[1536,256]{1,0:T(8,128)(2,1)} fusion(s32[1024]{0:T(1024)S(1)} %bitcast.126, bf16[1024,256]{1,0:T(8,128)(2,1)S(1)} %convolution_convert_fusion, bf16[]{:T(256)} %constant.9.clone.1), kind=kCustom, calls=%fused_computation.31 | custom fusion | bytes 786434 | tf_op jit(solution)/shard_map/scatter | solution.py:29
  162.9 1.5 pad_maximum_fusion
  164.5 6.3 %all_to_all.8 = bf16[32,1,36864]{2,1,0:T(2,128)(2,1)} reshape(bf16[1536,768]{1,0:T(8,128)(2,1)S(1)} %pad_maximum_fusion) | data formatting | bytes 4718592 | tf_op jit(solution)/shard_map/all_to_all | solution.py:37
  171.3 15.5 %reduce.1 = bf16[32,36864]{1,0:T(8,128)(2,1)S(1)} reduce(bf16[32,1,36864]{2,1,0:T(2,128)(2,1)} %all_to_all.8, bf16[]{:T(256)} %broadcast.201), dimensions={1}, to_apply=%all_to_all.8.reduce_sub_computation | reduce | bytes 4718594 | tf_op jit(solution)/shard_map/all_to_all | solution.py:37
  186.8 3.0 %reshape.232 = bf16[32,2,18432]{2,1,0:T(2,128)(2,1)} reshape(bf16[32,36864]{1,0:T(8,128)(2,1)S(1)} %reduce.1) | data formatting | bytes 4718592
  189.8 61.2 %all_to_all.10 = bf16[32,2,18432]{2,1,0:T(2,128)(2,1)S(1)} all-to-all(bf16[32,2,18432]{2,1,0:T(2,128)(2,1)} %reshape.232), channel_id=1, replica_groups=mesh['rows'=8,'serve'=4] {'rows','serve'}, dimensions={0} | all-to-all | bytes 4718592 | tf_op jit(solution)/shard_map/all_to_all | solution.py:37
  251.0 7.0 %reshape.233 = bf16[32,1,36864]{2,1,0:T(2,128)(2,1)} reshape(bf16[32,2,18432]{2,1,0:T(2,128)(2,1)S(1)} %all_to_all.10) | data formatting | bytes 4718592
  258.0 14.8 %reduce = bf16[32,36864]{1,0:T(8,128)(2,1)S(1)} reduce(bf16[32,1,36864]{2,1,0:T(2,128)(2,1)} %reshape.233, bf16[]{:T(256)} %constant.30), dimensions={1}, to_apply=%all_to_all.7.reduce_sub_computation | reduce | bytes 4718594 | tf_op jit(solution)/shard_map/all_to_all | solution.py:37
  272.8 2.5 reshape.200
  (59 shorter events, 17.9 us)
Async XLA Ops:
  6.5 12.8 %copy-start = (f32[3,1024,256]{2,1,0:T(8,128)S(1)}, f32[3,1024,256]{2,1,0:T(8,128)}, u32[]{:S(2)}) copy-start(f32[3,1024,256]{2,1,0:T(8,128)} %param.12) | copy-start | bytes 9437188
  6.5 12.7 %copy-start.4 = (s32[3,1024,1]{1,2,0:T(1,128)S(1)}, s32[3,1024,1]{1,2,0:T(1,128)}, u32[]{:S(2)}) copy-start(s32[3,1024,1]{1,2,0:T(1,128)} %param.17) | copy-start | bytes 36868
  6.5 12.8 %copy-start.2 = (f32[1024,32]{0,1:T(8,128)S(1)}, f32[1024,32]{0,1:T(8,128)}, u32[]{:S(2)}) copy-start(f32[1024,32]{0,1:T(8,128)} %param.9) | copy-start | bytes 393220
  6.5 136.7 %all-reduce.3.cloned.1.call-start = ((), (), s32[]{:S(2)}) async-start(), calls=%async_computation.1 | async-start | bytes 393216 | tf_op jit(solution)/shard_map/psum | solution.py:33
  8.7 4.0 %copy-start.10 = (pred[1024]{0:T(1024)(128)(4,1)}, pred[1024]{0:T(1024)(128)(4,1)S(1)}, u32[]{:S(2)}) copy-start(pred[1024]{0:T(1024)(128)(4,1)S(1)} %iota_compare_fusion.6) | copy-start | bytes 3076
  9.3 0.6 copy-start.11
  17.3 46.3 %copy-start.12 = (pred[1024]{0:T(1024)(128)(4,1)}, pred[1024]{0:T(1024)(128)(4,1)S(1)}, u32[]{:S(2)}) copy-start(pred[1024]{0:T(1024)(128)(4,1)S(1)} %iota_compare_fusion.8) | copy-start | bytes 3076
  19.3 53.4 %copy-start.6 = (s32[1,1024,1]{1,2,0:T(1,128)}, s32[1,1024,1]{1,2,0:T(1,128)S(1)}, u32[]{:S(2)}) copy-start(s32[1,1024,1]{1,2,0:T(1,128)S(1)} %get-tuple-element.12) | copy-start | bytes 12292
  19.3 81.8 %copy-start.8 = (s32[1,1024,1]{1,2,0:T(1,128)}, s32[1,1024,1]{1,2,0:T(1,128)S(1)}, u32[]{:S(2)}) copy-start(s32[1,1024,1]{1,2,0:T(1,128)S(1)} %get-tuple-element.11) | copy-start | bytes 12292
  19.3 81.8 %copy-start.9 = (s32[1,1024,1]{1,2,0:T(1,128)}, s32[1,1024,1]{1,2,0:T(1,128)S(1)}, u32[]{:S(2)}) copy-start(s32[1,1024,1]{1,2,0:T(1,128)S(1)} %get-tuple-element.10) | copy-start | bytes 12292
  62.3 1.3 copy-start.3
  109.3 9.6 %copy-start.7 = (s32[1,1024,1]{1,2,0:T(1,128)S(1)}, s32[1,1024,1]{1,2,0:T(1,128)}, u32[]{:S(2)}) copy-start(s32[1,1024,1]{1,2,0:T(1,128)} %copy-done.6) | copy-start | bytes 12292
  109.3 12.3 %copy-start.5 = (s32[3,1024,1]{1,2,0:T(1,128)S(1)}, s32[3,1024,1]{1,2,0:T(1,128)}, u32[]{:S(2)}) copy-start(s32[3,1024,1]{1,2,0:T(1,128)} %param.17) | copy-start | bytes 36868
  116.9 38.3 %copy-start.1 = (f32[1024,128]{1,0:T(8,128)S(1)}, f32[1024,128]{1,0:T(8,128)}, u32[]{:S(2)}) copy-start(f32[1024,128]{1,0:T(8,128)} %fusion) | copy-start | bytes 1572868
Sparse Core Ops, SparseCore 0:
  16.7 126.4 all-reduce.2
where the time goes:
time: 284 us; the launch traced here: 282 us
  blocking collectives  103 us (36%)
  other arithmetic  82.3 us (29%)
  local copies, waits for them, and re-layouts  47.2 us (17%)
  matrix products  20.4 us (7%)
  between operations  15.6 us (5%)
  waiting for transfers between devices  13.2 us (5%)
    all_to_all x1, blocking collectives, route_projected(): lax.all_to_all(buffer, ('rows', 'serve'), split_axis=0, concat_axis=0, ti...  61.2 us
    psum x1, blocking collectives, sum_gradients(): return lax.psum((totals[0], totals[1], totals[2]), ('rows', 'serve'))  42.1 us
    another operation x9, other arithmetic  37.4 us
    all_to_all x2, other arithmetic, route_projected(): lax.all_to_all(buffer, ('rows', 'serve'), split_axis=0, concat_axis=0, ti...  30.3 us
    dot_general x9, matrix products, highest_dot(): jnp.dot(left, right, precision=lax.Precision.HIGHEST, preferred_element_t...  20.4 us
    scatter x3, local copies, waits for them, and re-layouts, place_rows(): return empty.at[target].set(values, mode='drop')  17.1 us
    psum x1, waiting for transfers between devices, sum_gradients(): return lax.psum((totals[0], totals[1], totals[2]), ('rows', 'serve'))  13.2 us
    unnamed x29, local copies, waits for them, and re-layouts  11.6 us
  transfers between devices with their start and end apart: 1, of which 1 were waited for; matrix products, arithmetic and copies ran while one was open for 25% of the time, Pallas kernels for 0%

commit v1 on v0

v1 whole, which is shorter than its diff:
```python
import functools

import jax
import jax.numpy as jnp
from jax import lax
from jax.experimental import pallas as pl
from jax.experimental.pallas import tpu as pltpu
from jax.sharding import PartitionSpec as P

STEP_NORM = 16.0
ROW_RATE = 0.1
LANES = 128
CHUNK = 8
CODE_BITS = 14.9999
CODE_STEPS = 8.0
MIB = 1024 * 1024


def halves(value):
    high = value.astype(jnp.bfloat16)
    low = (value - high.astype(jnp.float32)).astype(jnp.bfloat16)
    return high, low


def contract(left, right, left_dim, right_dim):
    return lax.dot_general(
        left,
        right,
        (((left_dim,), (right_dim,)), ((), ())),
        preferred_element_type=jnp.float32,
    )


def row_top(values):
    return jnp.max(values, axis=1, keepdims=True)


def code_exponent(largest):
    return jnp.ceil(CODE_STEPS * jnp.log2(jnp.maximum(largest, 1e-30)))


def code(value, exponent):
    scaled = value * jnp.exp2(CODE_BITS - exponent * (1.0 / CODE_STEPS))
    return jnp.clip(jnp.floor(scaled + 0.5), -32767.0, 32767.0)


def code_scale(exponent):
    return jnp.exp2(exponent * (1.0 / CODE_STEPS) - CODE_BITS)


def whole(shape):
    return pl.BlockSpec(shape, lambda step: (0,) * len(shape))


def start_copies(sources, held, done):
    copies = [
        pltpu.make_async_copy(source, target, done.at[index])
        for index, (source, target) in enumerate(zip(sources, held))
    ]
    for copy in copies:
        copy.start()
    return copies


def share_codes(value):
    exponent = code_exponent(jnp.broadcast_to(row_top(jnp.abs(value)), value.shape))
    scaled = value * jnp.exp2(CODE_BITS + 8.0 - exponent * (1.0 / CODE_STEPS))
    whole_code = jnp.clip(jnp.floor(scaled + 0.5), -8388352.0, 8388352.0)
    upper = jnp.floor(whole_code * (1.0 / 256.0))
    lower = whole_code - 256.0 * upper
    upper = jnp.where(share_row(value.shape), exponent_row(exponent), upper)
    lower = lower[:, :LANES] * 256.0 + lower[:, LANES:] - 32768.0
    return jnp.concatenate([upper[:, :LANES], upper[:, LANES:], lower], axis=0)


def share_values(coded):
    upper = jnp.concatenate([coded[:CHUNK], coded[CHUNK : 2 * CHUNK]], axis=1)
    lower = coded[2 * CHUNK :] + 32768.0
    first = jnp.floor(lower * (1.0 / 256.0))
    lower = jnp.concatenate([first, lower - 256.0 * first], axis=1)
    scale = code_scale(exponent_column(upper)) * (1.0 / 256.0)
    return (upper * 256.0 + lower) * scale


def share_row(shape):
    return lax.broadcasted_iota(jnp.int32, shape, 0) == CHUNK - 1


def exponent_row(exponent):
    row = lax.broadcasted_iota(jnp.int32, exponent.shape, 0)
    lane = lax.broadcasted_iota(jnp.int32, exponent.shape, 1)
    return jnp.sum(jnp.where(row == lane, exponent, 0.0), axis=0, keepdims=True)


def exponent_column(coded):
    row = lax.broadcasted_iota(jnp.int32, coded.shape, 0)
    lane = lax.broadcasted_iota(jnp.int32, coded.shape, 1)
    exponents = jnp.where(row == lane, coded[CHUNK - 1 :], 0.0)
    return jnp.sum(exponents, axis=1, keepdims=True)


def owner_ranks(owner, live_count, device_count):
    slots = owner.shape[1]
    live = lax.broadcasted_iota(jnp.int32, (1, slots), 1) < live_count
    owner = jnp.where(live, owner, -1)
    named = lax.broadcasted_iota(jnp.int32, (device_count, slots), 0) == owner
    matched = jnp.where(named, 1.0, 0.0)
    parts = [matched[:, at : at + LANES] for at in range(0, slots, LANES)]
    stacked = jnp.concatenate(parts, axis=0).astype(jnp.bfloat16)
    row = lax.broadcasted_iota(jnp.int32, (LANES, 2 * LANES), 0)
    column = lax.broadcasted_iota(jnp.int32, (LANES, 2 * LANES), 1)
    counting = jnp.where((row < column) | (column >= LANES), 1.0, 0.0)
    sums = contract(stacked, counting.astype(jnp.bfloat16), 1, 0)
    running = jnp.zeros((device_count, LANES), jnp.float32)
    ranks = []
    for index, part in enumerate(parts):
        here = sums[index * device_count : (index + 1) * device_count]
        before = here[:, :LANES] + running
        ranks.append(jnp.sum(part * before, axis=0, keepdims=True))
        running = running + here[:, LANES:]
    return matched, jnp.concatenate(ranks, axis=1)


def rank_rows(rank, first, count):
    place = lax.broadcasted_iota(jnp.int32, (count, rank.shape[1]), 0) + first
    return jnp.where(place.astype(jnp.float32) == rank, 1.0, 0.0)


def moved_rows(table, projection, gradients):
    high, low = halves(projection)
    right = jnp.concatenate([high, low], axis=0)
    grad_high, grad_low = halves(gradients)
    product = contract(grad_high, right, 1, 1) + contract(grad_low, right, 1, 1)
    row_step = product[:, :LANES] + product[:, LANES:]
    return halves(table - ROW_RATE * row_step)


def in_lanes(pair, first, count):
    lane = lax.broadcasted_iota(jnp.int32, pair[0].shape, 1)
    kept = (lane >= first) & (lane < first + count)
    pair = [jnp.where(kept, half.astype(jnp.float32), 0.0) for half in pair]
    return jnp.concatenate(pair, axis=1).astype(jnp.bfloat16)


def widened(value, first):
    count, columns = value.shape
    above = [jnp.zeros((first, columns), value.dtype)] if first else []
    below = LANES - first - count
    below = [jnp.zeros((below, columns), value.dtype)] if below else []
    return jnp.concatenate(above + [value] + below, axis=0)


def packing(padded):
    share = 2 * CHUNK
    mid = share + padded // 2
    return share, mid, mid + padded // 3


def repeated(value, times):
    rest = LANES - times * value.shape[0]
    below = [jnp.zeros((rest, value.shape[1]), value.dtype)] if rest else []
    return jnp.concatenate([value] * times + below, axis=0)


def spread(column, rows):
    return jnp.broadcast_to(column, (rows, LANES))


def first_kernel(device_count, padded, group, counts, *refs):
    count = 8
    sources, out, held = refs[:count], refs[count], refs[count + 1 : 2 * count + 1]
    stacked, placed, ready, done, sent = refs[2 * count + 1 :]
    copies = start_copies(sources, held, done)
    owners, small, grads_small, mid, grads_mid, wide, proj_wide, grads_wide = held
    slots = wide.shape[0]
    w_small, w_mid, w_wide = small.shape[0], mid.shape[0], wide.shape[1]
    filled = w_wide + w_mid + w_small
    third = padded // 3

    def gradient_halves(grads):
        high, low = halves(grads[...])
        return jnp.concatenate([high, low], axis=1)

    def folded(product, width):
        out_width = product.shape[1] // 2
        upper = product[:width, :out_width] + product[:width, out_width:]
        return upper + (product[width:, :out_width] + product[width:, out_width:])

    def from_columns(table, grads, tier):
        width = table.shape[0]
        live = lax.broadcasted_iota(jnp.int32, (width, slots), 1) < counts[0, tier]
        high, low = halves(jnp.where(live, table[...], 0.0))
        left = jnp.concatenate([high, low], axis=0)
        return folded(contract(left, gradient_halves(grads), 1, 0), width)

    stacked[filled:, :] = jnp.zeros(
        (stacked.shape[0] - filled, stacked.shape[1]), jnp.float32
    )
    copies[0].wait()
    matched, rank = owner_ranks(owners[0], counts[0, 2], device_count)
    ranks = rank_rows(rank, 0, padded).astype(jnp.bfloat16)
    for copy in copies[1:3]:
        copy.wait()
    stacked[w_wide + w_mid : filled, :] = from_columns(small, grads_small, 0)
    for copy in copies[3:5]:
        copy.wait()
    stacked[w_wide : w_wide + w_mid, :] = from_columns(mid, grads_mid, 1)
    for copy in copies[5:8]:
        copy.wait()
    live = lax.broadcasted_iota(jnp.int32, (slots, w_wide), 0) < counts[0, 2]
    high, low = halves(jnp.where(live, wide[...], 0.0))
    left = jnp.concatenate([high, low], axis=1)
    product = contract(left, gradient_halves(grads_wide), 0, 0)
    stacked[0:w_wide, :] = folded(product, w_wide)
    moved = moved_rows(wide[...], proj_wide[...], grads_wide[...])
    placed[...] = jnp.concatenate(moved, axis=1)

    row = lax.broadcasted_iota(jnp.int32, (padded, LANES), 0) + CHUNK
    lane = lax.broadcasted_iota(jnp.int32, (padded, LANES), 1)
    diagonal = row == lane
    leaving = []
    for first in range(0, device_count, group):
        chosen = []
        for device in range(first, first + group):
            named = jnp.broadcast_to(matched[device : device + 1], (third, slots))
            named = named.astype(jnp.bfloat16)
            for at in range(3):
                chosen.append(ranks[at * third : (at + 1) * third] * named)
        pair = contract(jnp.concatenate(chosen, axis=0), placed[...], 1, 0)
        values = pair[:, :LANES] + pair[:, LANES:]
        top = spread(row_top(jnp.abs(values)), group * padded)
        exponent = code_exponent(top)
        coded = code(values, exponent).astype(jnp.int32)
        coded = coded.reshape(group, padded, LANES).astype(jnp.int16)
        ready[first : first + group, 0:padded, :] = coded
        exponent = exponent.reshape(group, padded, LANES)
        for device in range(first, first + group):
            start = device * (CHUNK - 1)
            share = share_codes(stacked[start : start + CHUNK])
            scales = jnp.where(diagonal, exponent[device - first], 0.0)
            scales = jnp.sum(scales, axis=0, keepdims=True)
            above = share[:CHUNK]
            spare = lax.broadcasted_iota(jnp.int32, above.shape, 1) >= CHUNK
            spare = spare & share_row(above.shape)
            share = jnp.concatenate(
                [jnp.where(spare, scales, above), share[CHUNK:]], axis=0
            )
            ready[device, padded:, :] = share.astype(jnp.int32).astype(jnp.int16)
        copy = pltpu.make_async_copy(
            ready.at[pl.ds(first, group)],
            out.at[pl.ds(first, group)],
            sent.at[first // group],
        )
        copy.start()
        leaving.append(copy)
    for copy in leaving:
        copy.wait()


def first_blocks(counts, small, mid, wide, grads, proj, owners, device_count, padded, group):
    slots, out_width = grads.shape[1:]
    block = (device_count, padded + 3 * CHUNK, LANES)

    def kernel(counts, owners, small, mid, wide, proj, grads, *rest):
        sources = (owners.at[pl.ds(2, 1)], small, grads.at[0], mid, grads.at[1])
        sources = sources + (wide, proj, grads.at[2])
        first_kernel(device_count, padded, group, counts, *sources, *rest)

    grad = pltpu.VMEM(grads.shape[1:], grads.dtype)
    held = [pltpu.VMEM((1,) + owners.shape[1:], owners.dtype)]
    held += [pltpu.VMEM(small.shape, small.dtype), grad]
    held += [pltpu.VMEM(mid.shape, mid.dtype), grad]
    held += [pltpu.VMEM(wide.shape, wide.dtype), pltpu.VMEM(proj.shape, proj.dtype), grad]
    return pl.pallas_call(
        kernel,
        out_shape=jax.ShapeDtypeStruct(block, jnp.int16),
        in_specs=[pl.BlockSpec(memory_space=pltpu.SMEM)]
        + [pl.BlockSpec(memory_space=pltpu.HBM)] * 6,
        out_specs=pl.BlockSpec(memory_space=pl.ANY),
        scratch_shapes=held
        + [
            pltpu.VMEM((device_count * CHUNK, out_width), jnp.float32),
            pltpu.VMEM((slots, 2 * LANES), jnp.bfloat16),
            pltpu.VMEM(block, jnp.int16),
            pltpu.SemaphoreType.DMA((8,)),
            pltpu.SemaphoreType.DMA((device_count // group,)),
        ],
        compiler_params=pltpu.CompilerParams(vmem_limit_bytes=56 * MIB),
        name="first_blocks",
    )(counts, owners, small, mid, wide, proj, grads)


def routing_kernel(device_count, padded, group, counts, *refs):
    count = 7
    sources, out, held = refs[:count], refs[count], refs[count + 1 : 2 * count + 1]
    placed, ready, done, sent = refs[2 * count + 1 :]
    copies = start_copies(sources, held, done)
    owners, small, proj_small, grads_small, mid, proj_mid, grads_mid = held
    w_small, w_mid = small.shape[0], mid.shape[0]
    slots = grads_mid.shape[0]
    half, third = padded // 2, padded // 3

    copies[0].wait()
    ranked = [
        owner_ranks(owners[tier], counts[0, tier], device_count) for tier in range(2)
    ]
    mid_ranks = [rank_rows(ranked[1][1], at * half, half) for at in range(2)]
    small_ranks = rank_rows(ranked[0][1], 0, padded).astype(jnp.bfloat16)
    for copy in copies[1:4]:
        copy.wait()
    table = repeated(small[...], 3).T
    moved = moved_rows(table, repeated(proj_small[...], 3), grads_small[...])
    for at in range(3):
        placed[2 + at] = in_lanes(moved, at * w_small, w_small)
    for copy in copies[4:7]:
        copy.wait()
    table = repeated(mid[...], 2).T
    moved = moved_rows(table, repeated(proj_mid[...], 2), grads_mid[...])
    for at in range(2):
        placed[at] = in_lanes(moved, at * w_mid, w_mid)

    def owner_row(tier, device, rows):
        return jnp.broadcast_to(ranked[tier][0][device : device + 1], (rows, slots))

    def picked(chosen, index):
        pair = contract(chosen, placed[index], 1, 0)
        return pair[:, :LANES] + pair[:, LANES:]

    spare = 3 * w_small
    leaving = []
    for first in range(0, device_count, group):
        devices = range(first, first + group)
        mid_rows = 0.0
        for at in range(2):
            chosen = [mid_ranks[at] * owner_row(1, device, half) for device in devices]
            chosen = jnp.concatenate(chosen, axis=0).astype(jnp.bfloat16)
            mid_rows = mid_rows + picked(chosen, at)
        named = [owner_row(0, device, third).astype(jnp.bfloat16) for device in devices]
        small_rows = 0.0
        for at in range(3):
            ranks = small_ranks[at * third : (at + 1) * third]
            chosen = jnp.concatenate([ranks * row for row in named], axis=0)
            small_rows = small_rows + picked(chosen, 2 + at)

        lane = lax.broadcasted_iota(jnp.int32, (group * half, LANES), 1)
        sizes = jnp.abs(mid_rows)
        mid_tops = [
            spread(row_top(jnp.where(side, sizes, 0.0)), group * half)
            for side in (lane < w_mid, lane >= w_mid)
        ]
        mid_top = jnp.where(lane < w_mid, mid_tops[0], mid_tops[1])
        lane = lax.broadcasted_iota(jnp.int32, (group * third, LANES), 1)
        sizes = jnp.abs(small_rows)
        by_slot = [top.reshape(group, half, LANES) for top in mid_tops]
        by_slot = jnp.concatenate(by_slot, axis=1)
        small_top = jnp.zeros((group * third, LANES), jnp.float32)
        for at in range(3):
            side = (lane >= at * w_small) & (lane < (at + 1) * w_small)
            top = row_top(jnp.where(side, sizes, 0.0))
            small_top = jnp.where(side | (lane == spare + at), top, small_top)
            top = by_slot[:, at * third : (at + 1) * third]
            top = top.reshape(group * third, LANES)
            small_top = jnp.where(lane == spare + 3 + at, top, small_top)

        small_exponent = code_exponent(small_top)
        small_code = code(small_rows, small_exponent)
        small_code = jnp.where(lane < spare, small_code, small_exponent)
        parts = (
            code(mid_rows, code_exponent(mid_top)).reshape(group, half, LANES),
            small_code.reshape(group, third, LANES),
        )
        coded = jnp.concatenate(parts, axis=1).astype(jnp.int32).astype(jnp.int16)
        ready[first : first + group] = coded
        copy = pltpu.make_async_copy(
            ready.at[pl.ds(first, group)],
            out.at[pl.ds(first, group)],
            sent.at[first // group],
        )
        copy.start()
        leaving.append(copy)
    for copy in leaving:
        copy.wait()


def routed_rows(
    counts, small, mid, grads, proj_small, proj_mid, owners, device_count, padded, group
):
    sources = (owners, small, proj_small, mid, proj_mid)
    block = (device_count, padded // 2 + padded // 3, LANES)
    held = [pltpu.VMEM(source.shape, source.dtype) for source in sources]
    for at in (3, 6):
        held.insert(at, pltpu.VMEM(grads.shape[1:], grads.dtype))

    def kernel(counts, owners, small, p_small, mid, p_mid, grads, *rest):
        sources = (owners, small, p_small, grads.at[0], mid, p_mid, grads.at[1])
        routing_kernel(device_count, padded, group, counts, *sources, *rest)

    return pl.pallas_call(
        kernel,
        out_shape=jax.ShapeDtypeStruct(block, jnp.int16),
        in_specs=[pl.BlockSpec(memory_space=pltpu.SMEM)]
        + [pl.BlockSpec(memory_space=pltpu.HBM)] * 6,
        out_specs=pl.BlockSpec(memory_space=pl.ANY),
        scratch_shapes=held
        + [
            pltpu.VMEM((5, grads.shape[1], 2 * LANES), jnp.bfloat16),
            pltpu.VMEM(block, jnp.int16),
            pltpu.SemaphoreType.DMA((7,)),
            pltpu.SemaphoreType.DMA((device_count // group,)),
        ],
        compiler_params=pltpu.CompilerParams(vmem_limit_bytes=56 * MIB),
        name="routed_rows",
    )(counts, *sources, grads)


def fetch_kernel(routed, out):
    out[...] = routed[...]


def fetched(routed):
    return pl.pallas_call(
        fetch_kernel,
        out_shape=jax.ShapeDtypeStruct(routed.shape, routed.dtype),
        compiler_params=pltpu.CompilerParams(vmem_limit_bytes=4 * MIB),
        name="fetched",
    )(routed)


def shares_kernel(pieces, routed, out):
    first = pieces.shape[1] - 3 * CHUNK
    summed = 0.0
    for device in range(pieces.shape[0]):
        summed = summed + share_values(pieces[device, first:].astype(jnp.float32))
    summed = jnp.where(share_row(summed.shape), 0.0, summed)
    exponent = code_exponent(jnp.broadcast_to(row_top(jnp.abs(summed)), summed.shape))
    coded = code(summed, exponent)
    coded = jnp.where(share_row(summed.shape), exponent_row(exponent), coded)
    coded = jnp.concatenate([coded[:, :LANES], coded[:, LANES:]], axis=0)
    coded = coded.astype(jnp.int32).astype(jnp.int16)
    share = 2 * CHUNK
    out[:, :share] = jnp.broadcast_to(coded[None], (out.shape[0],) + coded.shape)
    out[:, share:] = routed[...]


def with_shares(pieces, routed):
    device_count, rows, _ = routed.shape
    block = (device_count, 2 * CHUNK + rows, LANES)
    return pl.pallas_call(
        shares_kernel,
        out_shape=jax.ShapeDtypeStruct(block, routed.dtype),
        compiler_params=pltpu.CompilerParams(vmem_limit_bytes=8 * MIB),
        name="with_shares",
    )(pieces, routed)


def projecting_kernel(
    padded, everything, wide, rest, proj_small, proj_mid, proj_wide, out, weights
):
    group = rest.shape[0]
    w_small, w_mid, w_wide = proj_small.shape[0], proj_mid.shape[0], proj_wide.shape[0]
    out_width = proj_wide.shape[1]
    half, third = padded // 2, padded // 3
    share_end, mid_end, _ = packing(padded)

    @pl.when(pl.program_id(0) == 0)
    def _():
        shares = []
        for device in range(-(-(w_wide + w_mid + w_small) // (CHUNK - 1))):
            share = everything[device, 0:share_end, :].astype(jnp.float32)
            share = jnp.concatenate([share[:CHUNK], share[CHUNK:]], axis=1)
            scale = code_scale(exponent_column(share))
            shares.append((share * scale)[: CHUNK - 1])
        total = jnp.concatenate(shares, axis=0)
        tiers = (
            (proj_wide, 0, (0,)),
            (proj_mid, w_wide, (0, w_mid)),
            (proj_small, w_wide + w_mid, (0, w_small, 2 * w_small)),
        )
        index = 0
        for projection, start, places in tiers:
            part = total[start : start + projection.shape[0]]
            factor = STEP_NORM / jnp.sqrt(jnp.sum(part * part, keepdims=True) + 1e-06)
            fresh = projection[...] - factor * part
            for place in places:
                for piece in halves(widened(fresh, place)):
                    weights[index, 0:LANES] = piece * jnp.bfloat16(256.0)
                    weights[index, LANES:] = piece
                    index += 1

    def split_code(value):
        value = value.reshape(-1, LANES)
        upper = jnp.floor(value * (1.0 / 256.0))
        lower = value - 256.0 * upper
        return jnp.concatenate([upper, lower], axis=1).astype(jnp.bfloat16)

    def projected(left, index):
        product = contract(left, weights[2 * index], 1, 0)
        product = product + contract(left, weights[2 * index + 1], 1, 0)
        return product.reshape(group, -1, out_width)

    codes = rest[...].astype(jnp.float32)
    small_codes = codes[:, mid_end:]
    small_rows = split_code(small_codes)
    mid_rows = split_code(codes[:, share_end:mid_end])
    wide_codes = wide[...].astype(jnp.float32)
    wide_rows = split_code(wide_codes[:, 0:padded])
    row = lax.broadcasted_iota(jnp.int32, (group, padded, LANES), 1) + CHUNK
    lane = lax.broadcasted_iota(jnp.int32, (group, padded, LANES), 2)
    at = padded + CHUNK - 1
    scales = jnp.where(row == lane, wide_codes[:, at : at + 1], 0.0)
    wide_scale = code_scale(jnp.sum(scales, axis=2, keepdims=True))
    scales = code_scale(small_codes)
    spare = 3 * w_small
    slot_scales = [
        jnp.concatenate([scales[:, :, at : at + 1] for at in range(first, first + 3)], axis=1)
        for first in (spare, spare + 3)
    ]
    products = (
        ([projected(small_rows, 3 + at) for at in range(3)], slot_scales[0]),
        ([projected(mid_rows, 1 + at) for at in range(2)], slot_scales[1]),
        ([projected(wide_rows, 0)], wide_scale),
    )
    for tier, (parts, scale) in enumerate(products):
        product = jnp.concatenate(parts, axis=1) * scale
        product = product.astype(jnp.bfloat16).reshape(group * padded, out_width)
        out[:, tier * out_width : (tier + 1) * out_width] = product


def projected_rows(wide, rest, projections, padded, group):
    device_count = rest.shape[0]
    out_width = projections[2].shape[1]
    rows = group * padded
    return pl.pallas_call(
        functools.partial(projecting_kernel, padded),
        grid=(device_count // group,),
        out_shape=jax.ShapeDtypeStruct(
            (device_count * padded, 3 * out_width), jnp.bfloat16
        ),
        in_specs=[
            whole(rest.shape),
            pl.BlockSpec((group,) + wide.shape[1:], lambda step: (step, 0, 0)),
            pl.BlockSpec((group,) + rest.shape[1:], lambda step: (step, 0, 0)),
            *[whole(projection.shape) for projection in projections],
        ],
        out_specs=pl.BlockSpec((rows, 3 * out_width), lambda step: (step, 0)),
        scratch_shapes=[pltpu.VMEM((12, 2 * LANES, out_width), jnp.bfloat16)],
        compiler_params=pltpu.CompilerParams(vmem_limit_bytes=16 * MIB),
        name="projected_rows",
    )(rest, wide, rest, *projections)


def exchange(blocks):
    return lax.all_to_all(
        blocks, ("rows", "serve"), split_axis=0, concat_axis=0, tiled=True
    )


def local(
    rows_small, rows_mid, rows_wide, row_grads, proj_small, proj_mid, proj_wide, counts, owners
):
    device_count = lax.axis_size("rows") * lax.axis_size("serve")
    slots_here = rows_small.shape[0]
    capacity = max(2, slots_here // device_count + slots_here // (2 * device_count))
    padded = -(-capacity // 48) * 48
    out_width = row_grads.shape[2]
    group = 8 if device_count % 8 == 0 else 1
    small, mid = rows_small.T, rows_mid.T
    counts = counts.T
    owners = jnp.transpose(owners, (0, 2, 1))
    projections = (proj_small, proj_mid, proj_wide)
    sizes = (device_count, padded, 2 * group)
    first = first_blocks(
        counts, small, mid, rows_wide, row_grads, proj_wide, owners, *sizes
    )
    first = exchange(first)
    second = routed_rows(
        counts, small, mid, row_grads, proj_small, proj_mid, owners, *sizes
    )
    second = exchange(with_shares(first, fetched(second)))
    served = projected_rows(first, second, projections, padded, group)
    if padded != capacity:
        served = served.reshape(device_count, padded, 3 * out_width)[:, :capacity]
        served = served.reshape(device_count * capacity, 3 * out_width)
    return served


def solution(mesh):
    return jax.shard_map(
        local,
        mesh=mesh,
        in_specs=(
            P(("rows", "serve"), None),
            P(("rows", "serve"), None),
            P(("rows", "serve"), None),
            P(None, ("rows", "serve"), None),
            P(),
            P(),
            P(),
            P(None, ("rows", "serve")),
            P(None, ("rows", "serve"), None),
        ),
        out_specs=P(("rows", "serve"), None),
        check_vma=False,
    )
```

time: 284 us -> 51.5 us (0.18)
  blocking collectives: 103 us -> 17.5 us
  other arithmetic: 82.3 us -> 0 us
  local copies, waits for them, and re-layouts: 47.2 us -> 0.98 us
  matrix products: 20.4 us -> 0 us
  Pallas kernels: 0 us -> 15.8 us
  between operations: 15.6 us -> 0.07 us
  starting transfers between devices: 0.01 us -> 7.3 us
  waiting for transfers between devices: 13.2 us -> 9.53 us
    all_to_all x1, blocking collectives: 61.2 us -> 17.5 us  [exchange(): lax.all_to_all(blocks, ('rows', 'serve'), split_axis=0, concat_axis=0, ti...]
    psum x1 -> x0, blocking collectives: 42.1 us -> none  [sum_gradients(): return lax.psum((totals[0], totals[1], totals[2]), ('rows', 'serve'))]
    another operation x9 -> x0, other arithmetic: 37.4 us -> none
    all_to_all x2 -> x0, other arithmetic: 30.3 us -> none  [route_projected(): lax.all_to_all(buffer, ('rows', 'serve'), split_axis=0, concat_axis=0, ti...]
    dot_general x9 -> x0, matrix products: 20.4 us -> none  [highest_dot(): jnp.dot(left, right, precision=lax.Precision.HIGHEST, preferred_element_t...]
    scatter x3 -> x0, local copies, waits for them, and re-layouts: 17.1 us -> none  [place_rows(): return empty.at[target].set(values, mode='drop')]
    pallas_call x0 -> x5, Pallas kernels: none -> 15.8 us  [the longest x1 6.15 us: routed_rows(): pl.pallas_call(kernel, out_shape=jax.ShapeDtypeStruct(block, jnp.int16),...]
    psum x1 -> x0, waiting for transfers between devices: 13.2 us -> none  [sum_gradients(): return lax.psum((totals[0], totals[1], totals[2]), ('rows', 'serve'))]
  transfers between devices with their start and end apart: 1 -> 1, of which waited for: 1 -> 1; matrix products, arithmetic and copies ran while one was open for 25% -> 0% of each run, Pallas kernels for 0% -> 12%
where the time goes in v1:
time: 51.5 us; the launch traced here: 51.2 us
  blocking collectives  17.5 us (34%)
  Pallas kernels  15.8 us (31%)
  waiting for transfers between devices  9.53 us (19%)
  starting transfers between devices  7.3 us (14%)
  local copies, waits for them, and re-layouts  0.98 us (2%)
    all_to_all x1, blocking collectives, exchange(): lax.all_to_all(blocks, ('rows', 'serve'), split_axis=0, concat_axis=0, ti...  17.5 us
    all_to_all x1, waiting for transfers between devices, exchange(): lax.all_to_all(blocks, ('rows', 'serve'), split_axis=0, concat_axis=0, ti...  9.53 us
    all_to_all x1, starting transfers between devices, exchange(): lax.all_to_all(blocks, ('rows', 'serve'), split_axis=0, concat_axis=0, ti...  7.3 us
    pallas_call x1, Pallas kernels, routed_rows(): pl.pallas_call(kernel, out_shape=jax.ShapeDtypeStruct(block, jnp.int16),...  6.15 us
    pallas_call x1, Pallas kernels, first_blocks(): pl.pallas_call(kernel, out_shape=jax.ShapeDtypeStruct(block, jnp.int16),...  5.89 us
    pallas_call x1, Pallas kernels, projected_rows(): pl.pallas_call(functools.partial(projecting_kernel, padded), grid=(device...  3.5 us
  transfers between devices with their start and end apart: 1, of which 1 were waited for; matrix products, arithmetic and copies ran while one was open for 0% of the time, Pallas kernels for 12%

profile of v1, /device:TPU:0, one launch (start us, length us, event | category | flops | bytes accessed | tf_op | source)
XLA Modules:
  0.0 51.2 jit_solution(10692638507677878950)
XLA Ops:
  0.0 5.9 %first_blocks.1 = s16[32,72,128]{2,1,0:T(8,128)(2,1)} custom-call(s32[1,3]{1,0:T(1,128)} %bitcast.10, s32[3,1,1024]{2,1,0:T(1,128)} %bitcast.8, f32[32,1024]{1,0:T(8,128)} %bitcast.6, f32[64,1024]{1,0:T(8,128)} %bitcast.4, f32[1024,128]{1,0:T(8,128)} %wide.1, f32[128,256]{1,0:T(8,128)} %proj_wide.1, f32[3,1024,256]{2,1,0:T(8,128)} %grads.3), custom_call_target="tpu_custom_call" | custom-call | tf_op jit(solution)/shard_map/first_blocks/pallas_call | solution.py:274
  5.9 7.3 %all-to-all-start = ((s16[32,72,128]{2,1,0:T(8,128)(2,1)}), s16[32,72,128]{2,1,0:T(8,128)(2,1)S(1)}, u32[]{:S(2)}, u32[]{:S(2)}) async-start(s16[32,72,128]{2,1,0:T(8,128)(2,1)} %first_blocks.1), calls=%async_computation | async-start | bytes 1179648 | tf_op jit(solution)/shard_map/all_to_all | solution.py:553
  13.2 0.0 copy-start.1
  13.2 0.0 copy-start.2
  13.2 0.0 copy-start.3
  13.2 6.2 %routed_rows.1.routed = s16[32,40,128]{2,1,0:T(8,128)(2,1)} custom-call(s32[1,3]{1,0:T(1,128)} %bitcast.11, s32[3,1,1024]{2,1,0:T(1,128)} %bitcast.9, f32[32,1024]{1,0:T(8,128)} %bitcast.7, f32[32,256]{1,0:T(8,128)} %proj_small.1, f32[64,1024]{1,0:T(8,128)} %bitcast.5, f32[64,256]{1,0:T(8,128)} %proj_mid.1, f32[3,1024,256]{2,1,0:T(8,128)} %grads.3), custom_call_target="tpu_custom_call" | custom-call | tf_op jit(solution)/shard_map/routed_rows/pallas_call | solution.py:398
  19.4 0.0 copy-start
  19.4 1.0 %copy-done = s16[32,40,128]{2,1,0:T(8,128)(2,1)S(1)} copy-done((s16[32,40,128]{2,1,0:T(8,128)(2,1)S(1)}, s16[32,40,128]{2,1,0:T(8,128)(2,1)}, u32[]{:S(2)}) %copy-start) | copy-done | bytes 327704
  20.4 9.5 %all-to-all-done.pieces.wide = s16[32,72,128]{2,1,0:T(8,128)(2,1)S(1)} async-done(((s16[32,72,128]{2,1,0:T(8,128)(2,1)}), s16[32,72,128]{2,1,0:T(8,128)(2,1)S(1)}, u32[]{:S(2)}, u32[]{:S(2)}) %all-to-all-start) | async-done | bytes 589856 | tf_op jit(solution)/shard_map/all_to_all | solution.py:553
  29.9 0.2 with_shares.1
  30.2 17.5 %all_to_all.10.everything.rest = s16[32,56,128]{2,1,0:T(8,128)(2,1)S(1)} all-to-all(s16[32,56,128]{2,1,0:T(8,128)(2,1)S(1)} %with_shares.1), channel_id=1, replica_groups=mesh['rows'=8,'serve'=4] {'rows','serve'}, dimensions={0} | all-to-all | bytes 917504 | tf_op jit(solution)/shard_map/all_to_all | solution.py:553
  47.7 0.0 copy-done.1
  47.7 0.0 copy-done.2
  47.7 0.0 copy-done.3
  47.7 3.5 %projected_rows.1 = bf16[1536,768]{1,0:T(8,128)(2,1)} custom-call(s16[32,56,128]{2,1,0:T(8,128)(2,1)S(1)} %all_to_all.10.everything.rest, s16[32,72,128]{2,1,0:T(8,128)(2,1)S(1)} %all-to-all-done.pieces.wide, s16[32,56,128]{2,1,0:T(8,128)(2,1)S(1)} %all_to_all.10.everything.rest, f32[32,256]{1,0:T(8,128)S(1)} %copy-done.3, f32[64,256]{1,0:T(8,128)S(1)} %copy-done.2, ...), custom_call_target="tpu_custom_call" | custom-call | tf_op jit(solution)/shard_map/projected_rows/pallas_call | solution.py:533
  (1 shorter events, 0.0 us)
Async XLA Ops:
  5.9 24.0 %all-to-all-start = ((s16[32,72,128]{2,1,0:T(8,128)(2,1)}), s16[32,72,128]{2,1,0:T(8,128)(2,1)S(1)}, u32[]{:S(2)}, u32[]{:S(2)}) async-start(s16[32,72,128]{2,1,0:T(8,128)(2,1)} %first_blocks.1), calls=%async_computation | async-start | bytes 1179648 | tf_op jit(solution)/shard_map/all_to_all | solution.py:553
  13.2 34.4 %copy-start.1 = (f32[128,256]{1,0:T(8,128)S(1)}, f32[128,256]{1,0:T(8,128)}, u32[]{:S(2)}) copy-start(f32[128,256]{1,0:T(8,128)} %proj_wide.1) | copy-start | bytes 393220
  13.2 34.4 %copy-start.2 = (f32[64,256]{1,0:T(8,128)S(1)}, f32[64,256]{1,0:T(8,128)}, u32[]{:S(2)}) copy-start(f32[64,256]{1,0:T(8,128)} %proj_mid.1) | copy-start | bytes 196612
  13.2 34.4 %copy-start.3 = (f32[32,256]{1,0:T(8,128)S(1)}, f32[32,256]{1,0:T(8,128)}, u32[]{:S(2)}) copy-start(f32[32,256]{1,0:T(8,128)} %proj_small.1) | copy-start | bytes 98308
  19.4 1.0 %copy-start = (s16[32,40,128]{2,1,0:T(8,128)(2,1)S(1)}, s16[32,40,128]{2,1,0:T(8,128)(2,1)}, u32[]{:S(2)}) copy-start(s16[32,40,128]{2,1,0:T(8,128)(2,1)} %routed_rows.1.routed) | copy-start | bytes 983044
